TPU v7x, 128 devices: a whole 4x4x4 slice. The times are simulated.
128 devices in a mesh: ij: 8 (over z, core), ab: 16 (over y, x).
Axes of the slice: x: 4, y: 4, z: 4, core: 2. Of those that a mesh axis runs over, the one named last changes fastest.
Arguments:
- amplitudes: float32 [1024, 65536], P('ab', 'ij'), may hold values from -6 to 6
- integrals: float32 [4096, 65536], P('ab', 'ij'), may hold values from -0.03125 to 0.03125
Outputs:
- residual: float32 [1024, 4096], P('ij', 'ab')
All inputs are finite; a program needn't handle non-finite values.
Results may differ from a plain program's by a relative error of at most 0.000098.
Values sent between devices are 32-bit elements; how exact they have to be, the bound alone decides.
A program may use at most 128 MiB of HBM per device.

v0:
```python
import jax
import jax.numpy as jnp
from jax import lax
from jax.sharding import PartitionSpec as P


def contract(left, right):
    return lax.dot_general(
        left,
        right,
        (((1,), (1,)), ((), ())),
        precision=lax.Precision.HIGHEST,
        preferred_element_type=jnp.float32,
    )


def local(amplitudes, integrals):
    partial_value = contract(lax.all_gather(amplitudes, "ab", axis=0, tiled=True), integrals)
    return lax.psum_scatter(partial_value, "ij", scatter_dimension=0, tiled=True)


def solution(mesh):
    in_specs = (P("ab", "ij"), P("ab", "ij"))
    out_specs = P("ij", "ab")
    return jax.shard_map(local, mesh=mesh, in_specs=in_specs, out_specs=out_specs, check_vma=False)
```

profile of v0, /device:TPU:1, one launch (start us, length us, event | category | flops | bytes accessed | tf_op | source)
XLA Modules:
  0.0 277.3 jit_solution(10042054679053683926)
XLA Ops:
  6.5 0.0 all-gather.2.cloned.1.call-start
  6.5 0.7 all-gather.2.cloned.1.call-update
  7.3 0.0 reduce-scatter.2.cloned.1.call-start
  7.3 202.4 %all-gather.2.cloned.1.call-done = f32[1024,8192]{1,0:T(8,128)} async-done(((f32[64,8192]{1,0:T(8,128)}), f32[1024,8192]{1,0:T(8,128)}) %all-gather.2.cloned.1.call-update) | async-done | bytes 33554448 | tf_op jit(solution)/shard_map/all_gather | solution.py:18
  209.7 31.7 %fusion = f32[1024,256]{1,0:T(8,128)} fusion(f32[1024,8192]{1,0:T(8,128)} %all-gather.2.cloned.1.call-done, f32[256,8192]{1,0:T(8,128)} %param.3), kind=kOutput, calls=%fused_computation | convolution fusion | flops 25769803776 | bytes 42991616 | tf_op jit(solution)/shard_map/dot_general | solution.py:8
  241.4 0.0 reduce-scatter.2.cloned.1.call-update
  241.4 29.0 %reduce-scatter.2.cloned.1.call-done = f32[128,256]{1,0:T(8,128)} async-done(((f32[1024,256]{1,0:T(8,128)}), f32[128,256]{1,0:T(8,128)}) %reduce-scatter.2.cloned.1.call-update) | async-done | bytes 131088 | tf_op jit(solution)/shard_map/reduce_scatter | solution.py:19
Async XLA Ops:
  6.5 203.1 %all-gather.2.cloned.1.call-start = ((), (), s32[]{:S(2)}) async-start(), calls=%async_computation.1 | async-start | bytes 35651584 | tf_op jit(solution)/shard_map/all_gather | solution.py:18
  7.3 263.2 %reduce-scatter.2.cloned.1.call-start = ((), (), s32[]{:S(2)}) async-start(), calls=%async_computation.2 | async-start | bytes 1179648 | tf_op jit(solution)/shard_map/reduce_scatter | solution.py:19
Sparse Core Ops, SparseCore 0:
  9.5 200.1 all-gather.1
  241.5 28.8 reduce-scatter.1
where the time goes:
time: 280 us; the launch traced here: 277 us
  waiting for transfers between devices  232 us (83%)
  matrix products  31.7 us (11%)
  between operations  13.4 us (5%)
    all_gather x1, waiting for transfers between devices, local(): lax.all_gather(amplitudes, 'ab', axis=0, tiled=True)  202 us
    dot_general x1, matrix products, contract(): lax.dot_general(left, right, (((1,), (1,)), ((), ())), precision=lax.Prec...  31.7 us
    reduce_scatter x1, waiting for transfers between devices, local(): lax.psum_scatter(partial_value, 'ij', scatter_dimension=0, tiled=True)  29 us
  transfers between devices with their start and end apart: 2, of which 2 were waited for; matrix products, arithmetic and copies ran while one was open for 0% of the time, Pallas kernels for 0%

commit v1 on v0

v1 whole, which is shorter than its diff:
```python
import functools

import jax
import jax.numpy as jnp
from jax import lax
from jax.experimental import pallas as pl
from jax.experimental.pallas import tpu as pltpu
from jax.sharding import PartitionSpec as P

SIDE = 4
KQ = 2048
TROWS = 64
VROWS = 256
MZ = 256
CHUNKS = (64, 64, 64, 64)
VMEM_BYTES = 60 << 20


def place():
    ij, ab = lax.axis_index("ij"), lax.axis_index("ab")
    return ab % SIDE, ab // SIDE, ij // 2, ij % 2


def dot_nt(left, right):
    return lax.dot_general(left, right, (((1,), (1,)), ((), ())), preferred_element_type=jnp.float32)


def split(value):
    high = value.astype(jnp.bfloat16)
    return high, (value - high.astype(jnp.float32)).astype(jnp.bfloat16)


def kernel(t_ref, v_ref, o_ref, tbuf, vbuf, thi, tlo, vhi, vlo, ct, zbuf, zs, abuf, asum, cbuf,
           t_send, t_recv, g_send, g_recv, f_send, f_recv, v_send, v_recv, z_send, z_recv, a_send, a_recv,
           c_send, c_recv, local_sem):
    x, y, z, c = place()
    a = x * (1 - c) + y * c
    b = y * (1 - c) + x * c

    def device(a_to, b_to, z_to, c_to):
        x_to = a_to * (1 - c) + b_to * c
        y_to = b_to * (1 - c) + a_to * c
        return (z_to * 2 + c_to, y_to * SIDE + x_to)

    def slot(b_of, a_of):
        return (b_of * (1 - c) + a_of * c) * SIDE + a_of * (1 - c) + b_of * c

    def shifted(position, by):
        return (position + by + SIDE) % SIDE

    def along_a(by):
        return device(shifted(a, by), b, z, c)

    def along_b(by):
        return device(a, shifted(b, by), z, c)

    def along_z(by):
        return device(a, b, shifted(z, by), c)

    other_core = (z * 2 + 1 - c, y * SIDE + x)

    def columns(of):
        return pl.ds(pl.multiple_of(of * KQ, KQ), KQ)

    def remote(src, dst, send, recv, to):
        return pltpu.make_async_remote_copy(src_ref=src, dst_ref=dst, send_sem=send, recv_sem=recv, device_id=to,
                                            device_id_type=pl.DeviceIdType.MESH)

    barrier = pltpu.get_barrier_semaphore()
    peers = [along_a(j) for j in (1, 2, 3)] + [along_b(1), along_b(-1)] + [along_z(j) for j in (1, 2, 3)] + [other_core]
    for peer in peers:
        pl.semaphore_signal(barrier, inc=1, device_id=peer, device_id_type=pl.DeviceIdType.MESH)
    pl.semaphore_wait(barrier, len(peers))

    sent = []

    def go(copy):
        copy.start()
        sent.append(copy)
        return copy

    t_copies = {}
    for j in (1, 3, 2):
        t_copies[j] = go(remote(t_ref.at[:, columns(shifted(a, j))], tbuf.at[slot(b, a)], t_send.at[j], t_recv.at[j], along_a(j)))
    t_own = pltpu.make_async_copy(t_ref.at[:, columns(a)], tbuf.at[slot(b, a)], local_sem.at[0])
    t_own.start()
    v_own = pltpu.make_async_copy(v_ref.at[:, columns(a)], vbuf.at[a], local_sem.at[1])
    v_own.start()

    g_copies, f_copies = {}, {}

    def gather(j, src):
        dst = tbuf.at[slot(b, shifted(a, -j))]
        g_copies[j] = [go(remote(src, dst, g_send.at[2 * j + w], g_recv.at[2 * j + w], along_b(by))) for w, by in ((0, 1), (1, -1))]

    def forward(j):
        a_of = shifted(a, -j)
        f_copies[j] = []
        for w, by in ((0, 1), (1, -1)):
            g_copies[j][w].wait_recv()
            part = tbuf.at[slot(shifted(b, -by), a_of), pl.ds(w * (TROWS // 2), TROWS // 2)]
            f_copies[j].append(go(remote(part, part, f_send.at[2 * j + w], f_recv.at[2 * j + w], along_b(by))))

    v_copies = {}
    starts = [sum(CHUNKS[:k]) for k in range(len(CHUNKS))]

    def send_v(k):
        rows = pl.ds(starts[k], CHUNKS[k])
        v_copies[k] = [go(remote(v_ref.at[rows, columns(shifted(a, j))], vbuf.at[a, rows], v_send.at[3 * k + j - 1],
                                 v_recv.at[3 * k + j - 1], along_a(j))) for j in (1, 3, 2)]

    def convert_t(b_of, a_of):
        s = slot(b_of, a_of)
        rows = pl.ds(pl.multiple_of(s * TROWS, TROWS), TROWS)
        thi[rows, :], tlo[rows, :] = split(tbuf[s])

    gather(0, t_ref.at[:, columns(a)])
    send_v(0)
    t_copies[1].wait_recv()
    gather(1, tbuf.at[slot(b, shifted(a, -1))])
    t_copies[3].wait_recv()
    gather(3, tbuf.at[slot(b, shifted(a, -3))])
    forward(0)
    t_copies[2].wait_recv()
    gather(2, tbuf.at[slot(b, shifted(a, -2))])
    t_own.wait()
    convert_t(b, a)
    for j in (1, 3, 2):
        convert_t(b, shifted(a, -j))
    for j in (1, 3, 2):
        forward(j)
    send_v(1)
    for j in (0, 1, 3, 2):
        for by in (1, -1):
            convert_t(shifted(b, -by), shifted(a, -j))
    for j in (0, 1, 3, 2):
        for copy in f_copies[j]:
            copy.wait_recv()
        convert_t(shifted(b, 2), shifted(a, -j))
    v_own.wait()

    z_copies, a_copies, c_copies = {}, {}, {}

    def lanes_of(z_of):
        return pl.ds(pl.multiple_of(z_of * MZ, MZ), MZ)

    def multiply(k):
        size = CHUNKS[k]
        for copy in v_copies[k]:
            copy.wait_recv()
        for s in range(SIDE):
            rows = pl.ds(s * size, size)
            vhi[rows, :], vlo[rows, :] = split(vbuf[s, pl.ds(starts[k], size), :])
        n = pl.ds(0, SIDE * size)
        z_copies[k] = []
        for j in (1, 2, 3, 0):
            m = lanes_of(shifted(z, j))
            ct[k, n, m] = dot_nt(vhi[n, :], thi[m, :]) + dot_nt(vhi[n, :], tlo[m, :]) + dot_nt(vlo[n, :], thi[m, :])
            if j:
                z_copies[k].append(go(remote(ct.at[k, n, m], zbuf.at[k, j - 1, n], z_send.at[3 * k + j - 1],
                                             z_recv.at[3 * k + j - 1], along_z(j))))

    def reduce_z(k):
        size = CHUNKS[k]
        n = pl.ds(0, SIDE * size)
        for copy in z_copies[k]:
            copy.wait_recv()
        zs[k, n, :] = ct[k, n, lanes_of(z)] + zbuf[k, 0, n, :] + zbuf[k, 1, n, :] + zbuf[k, 2, n, :]
        a_copies[k] = []
        for j in (1, 3, 2):
            part = pl.ds(pl.multiple_of(shifted(a, j) * size, size), size)
            a_copies[k].append(go(remote(zs.at[k, part], abuf.at[k, j - 1, pl.ds(0, size)], a_send.at[3 * k + j - 1],
                                         a_recv.at[3 * k + j - 1], along_a(j))))

    def half(core):
        return pl.ds(pl.multiple_of(core * (MZ // 2), MZ // 2), MZ // 2)

    def reduce_a(k):
        size = CHUNKS[k]
        for copy in a_copies[k]:
            copy.wait_recv()
        own = zs[k, pl.ds(pl.multiple_of(a * size, size), size), :]
        rows = pl.ds(starts[k], size)
        q = pl.ds(0, size)
        asum[rows, :] = own + abuf[k, 0, q, :] + abuf[k, 1, q, :] + abuf[k, 2, q, :]
        c_copies[k] = go(remote(asum.at[rows, half(1 - c)], cbuf.at[rows], c_send.at[k], c_recv.at[k], other_core))

    def finish(k):
        c_copies[k].wait_recv()

    last = len(CHUNKS)
    for k in range(last + 3):
        if k < last:
            if k + 2 < last:
                send_v(k + 2)
            multiply(k)
        if 1 <= k <= last:
            reduce_z(k - 1)
        if 2 <= k <= last + 1:
            reduce_a(k - 2)
        if 3 <= k:
            finish(k - 3)
    o_ref[...] = (asum[:, half(c)] + cbuf[...]).T
    for copy in sent:
        copy.wait_send()


def local(amplitudes, integrals):
    steps, most = len(CHUNKS), max(CHUNKS)
    bf16, f32 = jnp.bfloat16, jnp.float32
    dma = pltpu.SemaphoreType.DMA
    return pl.pallas_call(
        kernel,
        out_shape=jax.ShapeDtypeStruct((MZ // 2, VROWS), f32),
        in_specs=[pl.BlockSpec(memory_space=pl.ANY)] * 2,
        out_specs=pl.BlockSpec(memory_space=pltpu.VMEM),
        scratch_shapes=[
            pltpu.VMEM((SIDE * SIDE, TROWS, KQ), f32),
            pltpu.VMEM((SIDE, VROWS, KQ), f32),
            pltpu.VMEM((SIDE * SIDE * TROWS, KQ), bf16),
            pltpu.VMEM((SIDE * SIDE * TROWS, KQ), bf16),
            pltpu.VMEM((SIDE * most, KQ), bf16),
            pltpu.VMEM((SIDE * most, KQ), bf16),
            pltpu.VMEM((steps, SIDE * most, SIDE * MZ), f32),
            pltpu.VMEM((steps, SIDE - 1, SIDE * most, MZ), f32),
            pltpu.VMEM((steps, SIDE * most, MZ), f32),
            pltpu.VMEM((steps, SIDE - 1, most, MZ), f32),
            pltpu.VMEM((VROWS, MZ), f32),
            pltpu.VMEM((VROWS, MZ // 2), f32),
            dma((SIDE,)), dma((SIDE,)),
            dma((2 * SIDE,)), dma((2 * SIDE,)),
            dma((2 * SIDE,)), dma((2 * SIDE,)),
            dma((3 * steps,)), dma((3 * steps,)),
            dma((3 * steps,)), dma((3 * steps,)),
            dma((3 * steps,)), dma((3 * steps,)),
            dma((steps,)), dma((steps,)),
            dma((2,)),
        ],
        compiler_params=pltpu.CompilerParams(collective_id=0, has_side_effects=True, vmem_limit_bytes=VMEM_BYTES),
        cost_estimate=pl.CostEstimate(flops=3 * 2 * 1024 * 1024 * KQ, bytes_accessed=10 << 20, transcendentals=0),
    )(amplitudes, integrals)


def solution(mesh):
    in_specs = (P("ab", "ij"), P("ab", "ij"))
    out_specs = P("ij", "ab")
    return jax.shard_map(local, mesh=mesh, in_specs=in_specs, out_specs=out_specs, check_vma=False)
```

time: 280 us -> 131 us (0.47)
  waiting for transfers between devices: 232 us -> 0 us
  Pallas kernels: 0 us -> 129 us
  matrix products: 31.7 us -> 0 us
  between operations: 13.4 us -> 0.01 us
    all_gather x1 -> x0, waiting for transfers between devices: 202 us -> none  [local(): lax.all_gather(amplitudes, 'ab', axis=0, tiled=True)]
    pallas_call x0 -> x1, Pallas kernels: none -> 129 us  [local(): pl.pallas_call(kernel, out_shape=jax.ShapeDtypeStruct((MZ // 2, VROWS), f...]
    dot_general x1 -> x0, matrix products: 31.7 us -> none  [contract(): lax.dot_general(left, right, (((1,), (1,)), ((), ())), precision=lax.Prec...]
    reduce_scatter x1 -> x0, waiting for transfers between devices: 29 us -> none  [local(): lax.psum_scatter(partial_value, 'ij', scatter_dimension=0, tiled=True)]
  transfers between devices with their start and end apart: 2 -> 0, of which waited for: 2 -> 0; matrix products, arithmetic and copies ran while one was open for 0% -> 0% of each run, Pallas kernels for 0% -> 0%
where the time goes in v1:
time: 131 us; the launch traced here: 130 us
  Pallas kernels  129 us (98%)
  local copies, waits for them, and re-layouts  1.57 us (1%)
    pallas_call x1, Pallas kernels, local(): pl.pallas_call(kernel, out_shape=jax.ShapeDtypeStruct((MZ // 2, VROWS), f...  129 us

profile of v1, /device:TPU:1, one launch (start us, length us, event | category | flops | bytes accessed | tf_op | source)
XLA Modules:
  0.0 130.5 jit_solution(8699557127142040178)
XLA Ops:
  0.0 128.9 %shard_map.28 = f32[128,256]{1,0:T(8,128)} custom-call(f32[64,8192]{1,0:T(8,128)} %t_ref.1, f32[256,8192]{1,0:T(8,128)} %v_ref.1), custom_call_target="tpu_custom_call" | custom-call | flops 12884901888 | bytes 10485760 | tf_op jit(solution)/shard_map/pallas_call | solution.py:212
  128.9 1.6 %copy.4 = f32[128,256]{1,0:T(8,128)} copy(f32[128,256]{1,0:T(8,128)} %shard_map.28) | data formatting | bytes 262144

commit v2 on v1

v2 whole, which is shorter than its diff:
```python
import functools

import jax
import jax.numpy as jnp
from jax import lax
from jax.experimental import pallas as pl
from jax.experimental.pallas import tpu as pltpu
from jax.sharding import PartitionSpec as P

SIDE = 4
KQ = 2048
TROWS = 64
VROWS = 256
MZ = 256
CHUNKS = (64, 64, 64, 32, 32)
A_FIRST = 2
VMEM_BYTES = 60 << 20


def place():
    ij, ab = lax.axis_index("ij"), lax.axis_index("ab")
    return ab % SIDE, ab // SIDE, ij // 2, ij % 2


def dot_nt(left, right):
    return lax.dot_general(left, right, (((1,), (1,)), ((), ())), preferred_element_type=jnp.float32)


def split(value):
    high = value.astype(jnp.bfloat16)
    return high, (value - high.astype(jnp.float32)).astype(jnp.bfloat16)


def kernel(t_ref, v_ref, o_ref, tbuf, vbuf, thi, tlo, vhl, ct, zbuf, zs, abuf, afirst, zdirect, asum, cbuf, out,
           t_send, t_recv, g_send, g_recv, f_send, f_recv, v_send, v_recv, z_send, z_recv, a_send, a_recv,
           d_send, d_recv, b_send, b_recv, c_send, c_recv, o_sem, local_sem):
    x, y, z, c = place()
    a = x * (1 - c) + y * c
    b = y * (1 - c) + x * c

    def device(a_to, b_to, z_to, c_to):
        x_to = a_to * (1 - c) + b_to * c
        y_to = b_to * (1 - c) + a_to * c
        return (z_to * 2 + c_to, y_to * SIDE + x_to)

    def slot(b_of, a_of):
        return (b_of * (1 - c) + a_of * c) * SIDE + a_of * (1 - c) + b_of * c

    def shifted(position, by):
        return (position + by + SIDE) % SIDE

    def along_a(by):
        return device(shifted(a, by), b, z, c)

    def along_b(by):
        return device(a, shifted(b, by), z, c)

    def along_z(by):
        return device(a, b, shifted(z, by), c)

    other_core = (z * 2 + 1 - c, y * SIDE + x)

    def columns(of):
        return pl.ds(pl.multiple_of(of * KQ, KQ), KQ)

    def remote(src, dst, send, recv, to):
        return pltpu.make_async_remote_copy(src_ref=src, dst_ref=dst, send_sem=send, recv_sem=recv, device_id=to,
                                            device_id_type=pl.DeviceIdType.MESH)

    barrier = pltpu.get_barrier_semaphore()
    peers = [along_a(j) for j in (1, 2, 3)] + [along_b(1), along_b(-1)] + [along_z(j) for j in (1, 2, 3)] + [other_core]
    peers += [device(a, b, shifted(z, j), 1 - c) for j in (1, 2, 3)]
    for peer in peers:
        pl.semaphore_signal(barrier, inc=1, device_id=peer, device_id_type=pl.DeviceIdType.MESH)
    pl.semaphore_wait(barrier, len(peers))

    sent = []

    def go(copy):
        copy.start()
        sent.append(copy)
        return copy

    t_copies = {}
    for j in (1, 3, 2):
        t_copies[j] = go(remote(t_ref.at[:, columns(shifted(a, j))], tbuf.at[slot(b, a)], t_send.at[j], t_recv.at[j], along_a(j)))
    t_own = pltpu.make_async_copy(t_ref.at[:, columns(a)], tbuf.at[slot(b, a)], local_sem.at[0])
    t_own.start()
    v_own = pltpu.make_async_copy(v_ref.at[:, columns(a)], vbuf.at[a], local_sem.at[1])
    v_own.start()

    g_copies = {}

    def gather(j, src):
        dst = tbuf.at[slot(b, shifted(a, -j))]
        g_copies[j] = [go(remote(src, dst, g_send.at[2 * j + w], g_recv.at[2 * j + w], along_b(by))) for w, by in ((0, 1), (1, -1))]

    def f_copy(j, w):
        by = 1 - 2 * w
        part = tbuf.at[slot(shifted(b, -by), shifted(a, -j)), pl.ds(w * (TROWS // 2), TROWS // 2)]
        return remote(part, part, f_send.at[2 * j + w], f_recv.at[2 * j + w], along_b(by))

    def forward(j):
        for w in (0, 1):
            g_copies[j][w].wait_recv()
            go(f_copy(j, w))

    v_copies = {}
    starts = [sum(CHUNKS[:k]) for k in range(len(CHUNKS))]

    def send_v(k):
        rows = pl.ds(starts[k], CHUNKS[k])
        v_copies[k] = [go(remote(v_ref.at[rows, columns(shifted(a, j))], vbuf.at[a, rows], v_send.at[3 * k + j - 1],
                                 v_recv.at[3 * k + j - 1], along_a(j))) for j in (1, 3, 2)]

    def convert_t(b_of, a_of):
        s = slot(b_of, a_of)
        rows = pl.ds(pl.multiple_of(s * TROWS, TROWS), TROWS)
        thi[rows, :], tlo[rows, :] = split(tbuf[s])

    def convert_sides(j):
        for by in (1, -1):
            convert_t(shifted(b, -by), shifted(a, -j))

    z_copies, a_copies, c_copies = {}, {}, {}

    def lanes_of(z_of):
        return pl.ds(pl.multiple_of(z_of * MZ, MZ), MZ)

    def half(core):
        return pl.ds(pl.multiple_of(core * (MZ // 2), MZ // 2), MZ // 2)

    last = len(CHUNKS)
    z_first = [k < last - A_FIRST for k in range(last)]

    def convert_v(k):
        size = CHUNKS[k]
        n = SIDE * size
        for copy in v_copies[k]:
            copy.wait_recv()

        @pl.loop(0, SIDE)
        def _(s):
            high, low = pl.ds(pl.multiple_of(s * size, size), size), pl.ds(pl.multiple_of(n + s * size, size), size)
            vhl[high, :], vhl[low, :] = split(vbuf[s, pl.ds(starts[k], size), :])

        a_copies[k] = []

    def multiply(k, m):
        n = SIDE * CHUNKS[k]
        both = dot_nt(vhl[pl.ds(0, 2 * n), :], thi[m, :])
        ct[k, pl.ds(0, n), m] = both[:n] + both[n:] + dot_nt(vhl[pl.ds(0, n), :], tlo[m, :])

    def z_copy(k, j):
        n = pl.ds(0, SIDE * CHUNKS[k])
        return remote(ct.at[k, n, lanes_of(shifted(z, j))], zbuf.at[k, j - 1, n], z_send.at[3 * k + j - 1],
                      z_recv.at[3 * k + j - 1], along_z(j))

    def wait_later(copies):
        sent.extend(copies)
        return copies

    def early_tiles():
        @pl.loop(0, SIDE)
        def _(i):
            j = i + i // 2 - 2 * (i // 3)
            for w in (0, 1):
                f_copy(j, w).wait_recv()
            convert_t(shifted(b, 2), shifted(a, -j))
            z_of = shifted(y, -j)
            multiply(0, lanes_of(z_of))
            by = shifted(z_of, -z)

            @pl.when(by != 0)
            def _():
                z_copy(0, by).start()

        z_copies[0] = wait_later([z_copy(0, j) for j in (1, 2, 3)])

    def a_first_copy(k, j, i):
        size, f = CHUNKS[k], k - last + A_FIRST
        m = lanes_of(shifted(z, j))
        part = pl.ds(pl.multiple_of(shifted(a, i) * size, size), size)
        at = 12 * f + 3 * j + i - 1
        return remote(ct.at[k, part, m], afirst.at[f, i - 1, pl.ds(0, size), m], b_send.at[at], b_recv.at[at], along_a(i))

    def all_tiles(k):
        convert_v(k)

        @pl.loop(0, SIDE)
        def _(step):
            j = (step + 1) % SIDE
            multiply(k, lanes_of(shifted(z, j)))
            if z_first[k]:
                @pl.when(step < SIDE - 1)
                def _():
                    z_copy(k, j).start()
            else:
                for i in (2, 1, 3):
                    a_first_copy(k, j, i).start()

        if z_first[k]:
            z_copies[k] = wait_later([z_copy(k, j) for j in (1, 2, 3)])
        else:
            z_copies[k] = []
            a_copies[k] = wait_later([a_first_copy(k, j, i) for j in (1, 2, 3, 0) for i in (2, 1, 3)])

    def reduce_first(k):
        size = CHUNKS[k]
        q = pl.ds(0, size)
        if z_first[k]:
            n = pl.ds(0, SIDE * size)
            for copy in z_copies[k]:
                copy.wait_recv()
            zs[k, n, :] = ct[k, n, lanes_of(z)] + zbuf[k, 0, n, :] + zbuf[k, 1, n, :] + zbuf[k, 2, n, :]
            for j in (2, 1, 3):
                part = pl.ds(pl.multiple_of(shifted(a, j) * size, size), size)
                a_copies[k].append(go(remote(zs.at[k, part], abuf.at[k, j - 1, q], a_send.at[3 * k + j - 1],
                                             a_recv.at[3 * k + j - 1], along_a(j))))
        else:
            f = k - last + A_FIRST
            own = pl.ds(pl.multiple_of(a * size, size), size)
            for i, j in enumerate((1, 2, 3, 0)):
                m = lanes_of(shifted(z, j))
                for copy in a_copies[k][3 * i : 3 * i + 3]:
                    copy.wait_recv()
                ct[k, own, m] = ct[k, own, m] + afirst[f, 0, q, m] + afirst[f, 1, q, m] + afirst[f, 2, q, m]
                for core in (0, 1):
                    if j or core:
                        at = 2 * j + core - 1
                        part = pl.ds(pl.multiple_of(shifted(z, j) * MZ + ((c + core) % 2) * (MZ // 2), MZ // 2), MZ // 2)
                        z_copies[k].append(go(remote(ct.at[k, own, part], zdirect.at[f, at, q], d_send.at[7 * f + at],
                                                     d_recv.at[7 * f + at], device(a, b, shifted(z, j), (c + core) % 2))))

    def write(k, value):
        rows = pl.ds(starts[k], CHUNKS[k])
        out[rows, :] = value
        written.append(pltpu.make_async_copy(out.at[rows], o_ref.at[rows], o_sem.at[k]))
        written[-1].start()

    written = []

    def reduce_second(k):
        size = CHUNKS[k]
        rows = pl.ds(starts[k], size)
        own = pl.ds(pl.multiple_of(a * size, size), size)
        q = pl.ds(0, size)
        if z_first[k]:
            for copy in a_copies[k]:
                copy.wait_recv()
            asum[rows, :] = zs[k, own, :] + abuf[k, 0, q, :] + abuf[k, 1, q, :] + abuf[k, 2, q, :]
            c_copies[k] = go(remote(asum.at[rows, half(1 - c)], cbuf.at[rows], c_send.at[k], c_recv.at[k], other_core))

    def finish(k):
        size = CHUNKS[k]
        rows = pl.ds(starts[k], size)
        q = pl.ds(0, size)
        if z_first[k]:
            c_copies[k].wait_recv()
            write(k, asum[rows, half(c)] + cbuf[rows, :])
        else:
            f = k - last + A_FIRST
            own = pl.ds(pl.multiple_of(a * size, size), size)
            value = ct[k, own, pl.ds(pl.multiple_of(z * MZ + c * (MZ // 2), MZ // 2), MZ // 2)]
            for copy in z_copies[k]:
                copy.wait_recv()
            for at in range(7):
                value += zdirect[f, at, q, :]
            write(k, value)

    gather(0, t_ref.at[:, columns(a)])
    send_v(0)
    t_copies[1].wait_recv()
    gather(1, tbuf.at[slot(b, shifted(a, -1))])
    t_copies[3].wait_recv()
    gather(3, tbuf.at[slot(b, shifted(a, -3))])
    forward(0)
    t_copies[2].wait_recv()
    gather(2, tbuf.at[slot(b, shifted(a, -2))])
    t_own.wait()
    v_own.wait()
    pl.loop(0, SIDE)(lambda j: convert_t(b, shifted(a, -j)))
    forward(1)
    forward(3)
    forward(2)
    send_v(1)
    pl.loop(0, SIDE)(convert_sides)
    convert_v(0)
    early_tiles()

    for k in range(1, last):
        for later in range(2 if k == 1 else k + 2, min(k + 3, last)):
            send_v(later)
        all_tiles(k)
        if 2 <= k < last - A_FIRST + 1:
            reduce_first(k - 2)
    for k in range(last - A_FIRST - 1, last):
        reduce_first(k)
    for k in range(last):
        reduce_second(k)
    for k in range(last):
        finish(k)
    for copy in sent:
        copy.wait_send()
    for copy in written:
        copy.wait()


def local(amplitudes, integrals):
    steps, most = len(CHUNKS), max(CHUNKS)
    bf16, f32 = jnp.bfloat16, jnp.float32
    dma = pltpu.SemaphoreType.DMA
    return pl.pallas_call(
        kernel,
        out_shape=jax.ShapeDtypeStruct((VROWS, MZ // 2), f32),
        in_specs=[pl.BlockSpec(memory_space=pl.ANY)] * 2,
        out_specs=pl.BlockSpec(memory_space=pl.ANY),
        scratch_shapes=[
            pltpu.VMEM((SIDE * SIDE, TROWS, KQ), f32),
            pltpu.VMEM((SIDE, VROWS, KQ), f32),
            pltpu.VMEM((SIDE * SIDE * TROWS, KQ), bf16),
            pltpu.VMEM((SIDE * SIDE * TROWS, KQ), bf16),
            pltpu.VMEM((2 * SIDE * most, KQ), bf16),
            pltpu.VMEM((steps, SIDE * most, SIDE * MZ), f32),
            pltpu.VMEM((steps, SIDE - 1, SIDE * most, MZ), f32),
            pltpu.VMEM((steps, SIDE * most, MZ), f32),
            pltpu.VMEM((steps, SIDE - 1, most, MZ), f32),
            pltpu.VMEM((A_FIRST, SIDE - 1, most, SIDE * MZ), f32),
            pltpu.VMEM((A_FIRST, 7, most, MZ // 2), f32),
            pltpu.VMEM((VROWS, MZ), f32),
            pltpu.VMEM((VROWS, MZ // 2), f32),
            pltpu.VMEM((VROWS, MZ // 2), f32),
            dma((SIDE,)), dma((SIDE,)),
            dma((2 * SIDE,)), dma((2 * SIDE,)),
            dma((2 * SIDE,)), dma((2 * SIDE,)),
            dma((3 * steps,)), dma((3 * steps,)),
            dma((3 * steps,)), dma((3 * steps,)),
            dma((3 * steps,)), dma((3 * steps,)),
            dma((7 * A_FIRST,)), dma((7 * A_FIRST,)),
            dma((12 * A_FIRST,)), dma((12 * A_FIRST,)),
            dma((steps,)), dma((steps,)),
            dma((steps,)),
            dma((2,)),
        ],
        compiler_params=pltpu.CompilerParams(collective_id=0, has_side_effects=True, vmem_limit_bytes=VMEM_BYTES),
        cost_estimate=pl.CostEstimate(flops=3 * 2 * 1024 * 1024 * KQ, bytes_accessed=10 << 20, transcendentals=0),
    )(amplitudes, integrals).T


def solution(mesh):
    in_specs = (P("ab", "ij"), P("ab", "ij"))
    out_specs = P("ij", "ab")
    return jax.shard_map(local, mesh=mesh, in_specs=in_specs, out_specs=out_specs, check_vma=False)
```

time: 131 us -> 117 us (0.89)
  Pallas kernels: 129 us -> 115 us
    pallas_call x1, Pallas kernels: 129 us -> 115 us  [local(): pl.pallas_call(kernel, out_shape=jax.ShapeDtypeStruct((VROWS, MZ // 2), f...]
    transpose x0 -> x1, local copies, waits for them, and re-layouts: none -> 1.66 us  [local(): return pl.pallas_call(kernel, out_shape=jax.ShapeDtypeStruct((VROWS, MZ /...]
    unnamed x1 -> x0, local copies, waits for them, and re-layouts: 1.57 us -> none
where the time goes in v2:
time: 117 us
  Pallas kernels  115 us (98%)
  local copies, waits for them, and re-layouts  1.66 us (1%)
    pallas_call x1, Pallas kernels, local(): pl.pallas_call(kernel, out_shape=jax.ShapeDtypeStruct((VROWS, MZ // 2), f...  115 us

profile of v2, /device:TPU:1, one launch (start us, length us, event | category | flops | bytes accessed | tf_op | source)
XLA Modules:
  0.0 116.5 jit_solution(6612010259478613280)
XLA Ops:
  0.0 114.9 %shard_map.28 = f32[256,128]{1,0:T(8,128)} custom-call(f32[64,8192]{1,0:T(8,128)} %t_ref.1, f32[256,8192]{1,0:T(8,128)} %v_ref.1), custom_call_target="tpu_custom_call" | custom-call | flops 12884901888 | bytes 10485760 | tf_op jit(solution)/shard_map/pallas_call | solution.py:313
  114.9 1.7 %copy.3 = f32[128,256]{1,0:T(8,128)} copy(f32[128,256]{0,1:T(8,128)} %bitcast.1) | data formatting | bytes 262144 | tf_op jit(solution)/shard_map/transpose | solution.py:347

commit v3 on v2

--- a/solution.py
+++ b/solution.py
@@ -31,9 +31,9 @@
     return high, (value - high.astype(jnp.float32)).astype(jnp.bfloat16)
 
 
-def kernel(t_ref, v_ref, o_ref, tbuf, vbuf, thi, tlo, vhl, ct, zbuf, zs, abuf, afirst, zdirect, asum, cbuf, out,
+def kernel(t_ref, v_ref, o_ref, tbuf, vbuf, thi, tlo, vhl, ct, zbuf, zs, abuf, afirst, zdirect, asum, cbuf,
            t_send, t_recv, g_send, g_recv, f_send, f_recv, v_send, v_recv, z_send, z_recv, a_send, a_recv,
-           d_send, d_recv, b_send, b_recv, c_send, c_recv, o_sem, local_sem):
+           d_send, d_recv, b_send, b_recv, c_send, c_recv, local_sem):
     x, y, z, c = place()
     a = x * (1 - c) + y * c
     b = y * (1 - c) + x * c
@@ -78,40 +78,48 @@
 
     def go(copy):
         copy.start()
-        sent.append(copy)
         return copy
+
+    def wait_sent(like, sem):
+        sent.append(remote(like, like, sem, sem, other_core))
+
+    def wait_received(like, sem):
+        remote(like, like, sem, sem, other_core).wait_recv()
 
     t_copies = {}
     for j in (1, 3, 2):
-        t_copies[j] = go(remote(t_ref.at[:, columns(shifted(a, j))], tbuf.at[slot(b, a)], t_send.at[j], t_recv.at[j], along_a(j)))
+        t_copies[j] = go(remote(t_ref.at[:, columns(shifted(a, j))], tbuf.at[slot(b, a)], t_send, t_recv.at[j - 1], along_a(j)))
+    wait_sent(vbuf.at[0, pl.ds(0, 3 * TROWS)], t_send)
     t_own = pltpu.make_async_copy(t_ref.at[:, columns(a)], tbuf.at[slot(b, a)], local_sem.at[0])
     t_own.start()
     v_own = pltpu.make_async_copy(v_ref.at[:, columns(a)], vbuf.at[a], local_sem.at[1])
     v_own.start()
 
     g_copies = {}
+    wait_sent(vbuf.at[pl.ds(0, 2)], g_send)
+    wait_sent(vbuf.at[0], f_send)
 
     def gather(j, src):
         dst = tbuf.at[slot(b, shifted(a, -j))]
-        g_copies[j] = [go(remote(src, dst, g_send.at[2 * j + w], g_recv.at[2 * j + w], along_b(by))) for w, by in ((0, 1), (1, -1))]
+        g_copies[j] = [go(remote(src, dst, g_send, g_recv.at[2 * j + w], along_b(by))) for w, by in ((0, 1), (1, -1))]
 
     def f_copy(j, w):
         by = 1 - 2 * w
         part = tbuf.at[slot(shifted(b, -by), shifted(a, -j)), pl.ds(w * (TROWS // 2), TROWS // 2)]
-        return remote(part, part, f_send.at[2 * j + w], f_recv.at[2 * j + w], along_b(by))
+        return remote(part, part, f_send, f_recv.at[j], along_b(by))
 
     def forward(j):
         for w in (0, 1):
             g_copies[j][w].wait_recv()
             go(f_copy(j, w))
 
-    v_copies = {}
+    wait_sent(vbuf.at[pl.ds(0, 3)], v_send)
     starts = [sum(CHUNKS[:k]) for k in range(len(CHUNKS))]
 
     def send_v(k):
         rows = pl.ds(starts[k], CHUNKS[k])
-        v_copies[k] = [go(remote(v_ref.at[rows, columns(shifted(a, j))], vbuf.at[a, rows], v_send.at[3 * k + j - 1],
-                                 v_recv.at[3 * k + j - 1], along_a(j))) for j in (1, 3, 2)]
+        for j in (1, 3, 2):
+            go(remote(v_ref.at[rows, columns(shifted(a, j))], vbuf.at[a, rows], v_send, v_recv.at[k], along_a(j)))
 
     def convert_t(b_of, a_of):
         s = slot(b_of, a_of)
@@ -122,7 +130,7 @@
         for by in (1, -1):
             convert_t(shifted(b, -by), shifted(a, -j))
 
-    z_copies, a_copies, c_copies = {}, {}, {}
+    c_copies = {}
 
     def lanes_of(z_of):
         return pl.ds(pl.multiple_of(z_of * MZ, MZ), MZ)
@@ -136,16 +144,13 @@
     def convert_v(k):
         size = CHUNKS[k]
         n = SIDE * size
-        for copy in v_copies[k]:
-            copy.wait_recv()
+        wait_received(vbuf.at[pl.ds(0, 3), pl.ds(starts[k], size)], v_recv.at[k])
 
         @pl.loop(0, SIDE)
         def _(s):
             high, low = pl.ds(pl.multiple_of(s * size, size), size), pl.ds(pl.multiple_of(n + s * size, size), size)
             vhl[high, :], vhl[low, :] = split(vbuf[s, pl.ds(starts[k], size), :])
 
-        a_copies[k] = []
-
     def multiply(k, m):
         n = SIDE * CHUNKS[k]
         both = dot_nt(vhl[pl.ds(0, 2 * n), :], thi[m, :])
@@ -153,19 +158,13 @@
 
     def z_copy(k, j):
         n = pl.ds(0, SIDE * CHUNKS[k])
-        return remote(ct.at[k, n, lanes_of(shifted(z, j))], zbuf.at[k, j - 1, n], z_send.at[3 * k + j - 1],
-                      z_recv.at[3 * k + j - 1], along_z(j))
-
-    def wait_later(copies):
-        sent.extend(copies)
-        return copies
+        return remote(ct.at[k, n, lanes_of(shifted(z, j))], zbuf.at[k, j - 1, n], z_send.at[k], z_recv.at[k], along_z(j))
 
     def early_tiles():
         @pl.loop(0, SIDE)
         def _(i):
             j = i + i // 2 - 2 * (i // 3)
-            for w in (0, 1):
-                f_copy(j, w).wait_recv()
+            wait_received(tbuf.at[0], f_recv.at[j])
             convert_t(shifted(b, 2), shifted(a, -j))
             z_of = shifted(y, -j)
             multiply(0, lanes_of(z_of))
@@ -175,14 +174,14 @@
             def _():
                 z_copy(0, by).start()
 
-        z_copies[0] = wait_later([z_copy(0, j) for j in (1, 2, 3)])
+        wait_sent(zbuf.at[0, :, pl.ds(0, SIDE * CHUNKS[0])], z_send.at[0])
 
     def a_first_copy(k, j, i):
         size, f = CHUNKS[k], k - last + A_FIRST
         m = lanes_of(shifted(z, j))
         part = pl.ds(pl.multiple_of(shifted(a, i) * size, size), size)
-        at = 12 * f + 3 * j + i - 1
-        return remote(ct.at[k, part, m], afirst.at[f, i - 1, pl.ds(0, size), m], b_send.at[at], b_recv.at[at], along_a(i))
+        return remote(ct.at[k, part, m], afirst.at[f, i - 1, pl.ds(0, size), m], b_send.at[f],
+                      b_recv.at[SIDE * f + j], along_a(i))
 
     def all_tiles(k):
         convert_v(k)
@@ -200,45 +199,40 @@
                     a_first_copy(k, j, i).start()
 
         if z_first[k]:
-            z_copies[k] = wait_later([z_copy(k, j) for j in (1, 2, 3)])
+            wait_sent(zbuf.at[k, :, pl.ds(0, SIDE * CHUNKS[k])], z_send.at[k])
         else:
-            z_copies[k] = []
-            a_copies[k] = wait_later([a_first_copy(k, j, i) for j in (1, 2, 3, 0) for i in (2, 1, 3)])
+            f = k - last + A_FIRST
+            wait_sent(afirst.at[f, :, pl.ds(0, CHUNKS[k])], b_send.at[f])
 
     def reduce_first(k):
         size = CHUNKS[k]
         q = pl.ds(0, size)
         if z_first[k]:
             n = pl.ds(0, SIDE * size)
-            for copy in z_copies[k]:
-                copy.wait_recv()
+            wait_received(zbuf.at[k, :, n], z_recv.at[k])
             zs[k, n, :] = ct[k, n, lanes_of(z)] + zbuf[k, 0, n, :] + zbuf[k, 1, n, :] + zbuf[k, 2, n, :]
             for j in (2, 1, 3):
                 part = pl.ds(pl.multiple_of(shifted(a, j) * size, size), size)
-                a_copies[k].append(go(remote(zs.at[k, part], abuf.at[k, j - 1, q], a_send.at[3 * k + j - 1],
-                                             a_recv.at[3 * k + j - 1], along_a(j))))
+                go(remote(zs.at[k, part], abuf.at[k, j - 1, q], a_send.at[k], a_recv.at[k], along_a(j)))
+            wait_sent(abuf.at[k, :, q], a_send.at[k])
         else:
             f = k - last + A_FIRST
             own = pl.ds(pl.multiple_of(a * size, size), size)
-            for i, j in enumerate((1, 2, 3, 0)):
+            for j in (1, 2, 3, 0):
                 m = lanes_of(shifted(z, j))
-                for copy in a_copies[k][3 * i : 3 * i + 3]:
-                    copy.wait_recv()
+                wait_received(afirst.at[f, :, q, m], b_recv.at[SIDE * f + j])
                 ct[k, own, m] = ct[k, own, m] + afirst[f, 0, q, m] + afirst[f, 1, q, m] + afirst[f, 2, q, m]
                 for core in (0, 1):
                     if j or core:
                         at = 2 * j + core - 1
                         part = pl.ds(pl.multiple_of(shifted(z, j) * MZ + ((c + core) % 2) * (MZ // 2), MZ // 2), MZ // 2)
-                        z_copies[k].append(go(remote(ct.at[k, own, part], zdirect.at[f, at, q], d_send.at[7 * f + at],
-                                                     d_recv.at[7 * f + at], device(a, b, shifted(z, j), (c + core) % 2))))
+                        go(remote(ct.at[k, own, part], zdirect.at[f, at, q], d_send.at[f], d_recv.at[f],
+                                  device(a, b, shifted(z, j), (c + core) % 2)))
+            wait_sent(zdirect.at[f, :, q], d_send.at[f])
 
     def write(k, value):
         rows = pl.ds(starts[k], CHUNKS[k])
-        out[rows, :] = value
-        written.append(pltpu.make_async_copy(out.at[rows], o_ref.at[rows], o_sem.at[k]))
-        written[-1].start()
-
-    written = []
+        o_ref[rows, :] = value
 
     def reduce_second(k):
         size = CHUNKS[k]
@@ -246,10 +240,10 @@
         own = pl.ds(pl.multiple_of(a * size, size), size)
         q = pl.ds(0, size)
         if z_first[k]:
-            for copy in a_copies[k]:
-                copy.wait_recv()
+            wait_received(abuf.at[k, :, q], a_recv.at[k])
             asum[rows, :] = zs[k, own, :] + abuf[k, 0, q, :] + abuf[k, 1, q, :] + abuf[k, 2, q, :]
             c_copies[k] = go(remote(asum.at[rows, half(1 - c)], cbuf.at[rows], c_send.at[k], c_recv.at[k], other_core))
+            sent.append(c_copies[k])
 
     def finish(k):
         size = CHUNKS[k]
@@ -262,8 +256,7 @@
             f = k - last + A_FIRST
             own = pl.ds(pl.multiple_of(a * size, size), size)
             value = ct[k, own, pl.ds(pl.multiple_of(z * MZ + c * (MZ // 2), MZ // 2), MZ // 2)]
-            for copy in z_copies[k]:
-                copy.wait_recv()
+            wait_received(zdirect.at[f, :, q], d_recv.at[f])
             for at in range(7):
                 value += zdirect[f, at, q, :]
             write(k, value)
@@ -302,8 +295,6 @@
         finish(k)
     for copy in sent:
         copy.wait_send()
-    for copy in written:
-        copy.wait()
 
 
 def local(amplitudes, integrals):
@@ -312,9 +303,9 @@
     dma = pltpu.SemaphoreType.DMA
     return pl.pallas_call(
         kernel,
-        out_shape=jax.ShapeDtypeStruct((VROWS, MZ // 2), f32),
+        out_shape=pltpu.VMEM((VROWS, MZ // 2), f32),
         in_specs=[pl.BlockSpec(memory_space=pl.ANY)] * 2,
-        out_specs=pl.BlockSpec(memory_space=pl.ANY),
+        out_specs=pl.BlockSpec(memory_space=pltpu.VMEM),
         scratch_shapes=[
             pltpu.VMEM((SIDE * SIDE, TROWS, KQ), f32),
             pltpu.VMEM((SIDE, VROWS, KQ), f32),
@@ -329,17 +320,15 @@
             pltpu.VMEM((A_FIRST, 7, most, MZ // 2), f32),
             pltpu.VMEM((VROWS, MZ), f32),
             pltpu.VMEM((VROWS, MZ // 2), f32),
-            pltpu.VMEM((VROWS, MZ // 2), f32),
-            dma((SIDE,)), dma((SIDE,)),
-            dma((2 * SIDE,)), dma((2 * SIDE,)),
-            dma((2 * SIDE,)), dma((2 * SIDE,)),
-            dma((3 * steps,)), dma((3 * steps,)),
-            dma((3 * steps,)), dma((3 * steps,)),
-            dma((3 * steps,)), dma((3 * steps,)),
-            dma((7 * A_FIRST,)), dma((7 * A_FIRST,)),
-            dma((12 * A_FIRST,)), dma((12 * A_FIRST,)),
-            dma((steps,)), dma((steps,)),
-            dma((steps,)),
+            dma(()), dma((SIDE - 1,)),
+            dma(()), dma((2 * SIDE,)),
+            dma(()), dma((SIDE,)),
+            dma(()), dma((steps,)),
+            dma((steps - A_FIRST,)), dma((steps - A_FIRST,)),
+            dma((steps - A_FIRST,)), dma((steps - A_FIRST,)),
+            dma((A_FIRST,)), dma((A_FIRST,)),
+            dma((A_FIRST,)), dma((SIDE * A_FIRST,)),
+            dma((steps - A_FIRST,)), dma((steps - A_FIRST,)),
             dma((2,)),
         ],
         compiler_params=pltpu.CompilerParams(collective_id=0, has_side_effects=True, vmem_limit_bytes=VMEM_BYTES),

time: 117 us -> 114 us (0.974)
  Pallas kernels: 115 us -> 113 us
    pallas_call x1, Pallas kernels: 115 us -> 113 us  [local(): pl.pallas_call(kernel, out_shape=pltpu.VMEM((VROWS, MZ // 2), f32), in_sp...]
where the time goes in v3:
time: 114 us
  Pallas kernels  113 us (99%)
    pallas_call x1, Pallas kernels, local(): pl.pallas_call(kernel, out_shape=pltpu.VMEM((VROWS, MZ // 2), f32), in_sp...  113 us

profile of v3, /device:TPU:1, one launch (start us, length us, event | category | flops | bytes accessed | tf_op | source)
XLA Modules:
  0.0 114.1 jit_solution(2978499034104937917)
XLA Ops:
  0.0 113.4 %shard_map.28 = f32[256,128]{1,0:T(8,128)S(1)} custom-call(f32[64,8192]{1,0:T(8,128)} %t_ref.1, f32[256,8192]{1,0:T(8,128)} %v_ref.1), custom_call_target="tpu_custom_call" | custom-call | flops 12884901888 | bytes 10485760 | tf_op jit(solution)/shard_map/pallas_call | solution.py:304
  113.4 0.8 copy.3

commit v4 on v3

--- a/solution.py
+++ b/solution.py
@@ -13,6 +13,7 @@
 VROWS = 256
 MZ = 256
 CHUNKS = (64, 64, 64, 32, 32)
+LATE = 1
 A_FIRST = 2
 VMEM_BYTES = 60 << 20
 
@@ -31,9 +32,9 @@
     return high, (value - high.astype(jnp.float32)).astype(jnp.bfloat16)
 
 
-def kernel(t_ref, v_ref, o_ref, tbuf, vbuf, thi, tlo, vhl, ct, zbuf, zs, abuf, afirst, zdirect, asum, cbuf,
+def kernel(t_ref, v_ref, o_ref, tbuf, vbuf, thi, tlo, vhl, ct, zh, zbuf, zs, abuf, afirst, zdirect,
            t_send, t_recv, g_send, g_recv, f_send, f_recv, v_send, v_recv, z_send, z_recv, a_send, a_recv,
-           d_send, d_recv, b_send, b_recv, c_send, c_recv, local_sem):
+           d_send, d_recv, b_send, b_recv, h_send, h_recv, local_sem):
     x, y, z, c = place()
     a = x * (1 - c) + y * c
     b = y * (1 - c) + x * c
@@ -70,6 +71,7 @@
     barrier = pltpu.get_barrier_semaphore()
     peers = [along_a(j) for j in (1, 2, 3)] + [along_b(1), along_b(-1)] + [along_z(j) for j in (1, 2, 3)] + [other_core]
     peers += [device(a, b, shifted(z, j), 1 - c) for j in (1, 2, 3)]
+    peers += [device(a, shifted(b, j), z, 1 - c) for j in (1, 2, 3)]
     for peer in peers:
         pl.semaphore_signal(barrier, inc=1, device_id=peer, device_id_type=pl.DeviceIdType.MESH)
     pl.semaphore_wait(barrier, len(peers))
@@ -121,6 +123,13 @@
         for j in (1, 3, 2):
             go(remote(v_ref.at[rows, columns(shifted(a, j))], vbuf.at[a, rows], v_send, v_recv.at[k], along_a(j)))
 
+    def send_v_half(h):
+        k = len(CHUNKS) - 1
+        rows = pl.ds(starts[k], CHUNKS[k])
+        for j in (1, 3, 2):
+            src = pl.ds(pl.multiple_of(shifted(a, j) * KQ + h * (KQ // 2), KQ // 2), KQ // 2)
+            go(remote(v_ref.at[rows, src], vbuf.at[a, rows, pl.ds(h * (KQ // 2), KQ // 2)], v_send, v_recv.at[k + h], along_a(j)))
+
     def convert_t(b_of, a_of):
         s = slot(b_of, a_of)
         rows = pl.ds(pl.multiple_of(s * TROWS, TROWS), TROWS)
@@ -130,7 +139,6 @@
         for by in (1, -1):
             convert_t(shifted(b, -by), shifted(a, -j))
 
-    c_copies = {}
 
     def lanes_of(z_of):
         return pl.ds(pl.multiple_of(z_of * MZ, MZ), MZ)
@@ -183,23 +191,66 @@
         return remote(ct.at[k, part, m], afirst.at[f, i - 1, pl.ds(0, size), m], b_send.at[f],
                       b_recv.at[SIDE * f + j], along_a(i))
 
-    def all_tiles(k):
-        convert_v(k)
+    def half_tiles(k, h):
+        size = CHUNKS[k]
+        n = SIDE * size
+        lanes = pl.ds(h * (KQ // 2), KQ // 2)
+        wait_received(vbuf.at[pl.ds(0, 3), pl.ds(starts[k], size), lanes], v_recv.at[k + h])
+
+        @pl.loop(0, SIDE)
+        def _(s):
+            high, low = pl.ds(pl.multiple_of(s * size, size), size), pl.ds(pl.multiple_of(n + s * size, size), size)
+            vhl[high, lanes], vhl[low, lanes] = split(vbuf[s, pl.ds(starts[k], size), lanes])
 
         @pl.loop(0, SIDE)
         def _(step):
             j = (step + 1) % SIDE
+            m = lanes_of(shifted(z, j))
+            both = dot_nt(vhl[pl.ds(0, 2 * n), lanes], thi[m, lanes])
+            value = both[:n] + both[n:] + dot_nt(vhl[pl.ds(0, n), lanes], tlo[m, lanes])
+            if h == 0:
+                ct[k, pl.ds(0, n), m] = value
+            else:
+                ct[k, pl.ds(0, n), m] += value
+                for i in (2, 1, 3):
+                    a_first_copy(k, j, i).start()
+
+    def all_tiles(k):
+        if k == last - 1:
+            half_tiles(k, 0)
+            half_tiles(k, 1)
+            wait_sent(afirst.at[k - last + A_FIRST, :, pl.ds(0, CHUNKS[k])], b_send.at[k - last + A_FIRST])
+            return
+        convert_v(k)
+
+        n = SIDE * CHUNKS[k]
+
+        def opposite_half(w):
+            part = ct.at[k, pl.ds(w * n // 2, n // 2), lanes_of(shifted(z, 2))]
+            return remote(part, zh.at[k, w, pl.ds(0, n // 2)], h_send.at[k], h_recv.at[k], along_z(1 - 2 * w))
+
+        @pl.loop(0, SIDE)
+        def _(step):
+            j = (step + 2) % SIDE if z_first[k] else (step + 1) % SIDE
             multiply(k, lanes_of(shifted(z, j)))
             if z_first[k]:
-                @pl.when(step < SIDE - 1)
+                @pl.when(step == 0)
                 def _():
-                    z_copy(k, j).start()
+                    for w in (0, 1):
+                        opposite_half(w).start()
             else:
                 for i in (2, 1, 3):
                     a_first_copy(k, j, i).start()
 
         if z_first[k]:
-            wait_sent(zbuf.at[k, :, pl.ds(0, SIDE * CHUNKS[k])], z_send.at[k])
+            wait_sent(zh.at[k, :, pl.ds(0, n // 2)], h_send.at[k])
+            wait_received(zh.at[k, :, pl.ds(0, n // 2)], h_recv.at[k])
+            for w in (0, 1):
+                m = lanes_of(shifted(z, 1 - 2 * w))
+                rows = pl.ds(0, n)
+                ct[k, pl.ds(w * n // 2, n // 2), m] += zh[k, w, pl.ds(0, n // 2), :]
+                go(remote(ct.at[k, rows, m], zbuf.at[k, w, rows], z_send.at[k], z_recv.at[k], along_z(1 - 2 * w)))
+            wait_sent(zbuf.at[k, pl.ds(0, 2), pl.ds(0, n)], z_send.at[k])
         else:
             f = k - last + A_FIRST
             wait_sent(afirst.at[f, :, pl.ds(0, CHUNKS[k])], b_send.at[f])
@@ -209,11 +260,18 @@
         q = pl.ds(0, size)
         if z_first[k]:
             n = pl.ds(0, SIDE * size)
-            wait_received(zbuf.at[k, :, n], z_recv.at[k])
-            zs[k, n, :] = ct[k, n, lanes_of(z)] + zbuf[k, 0, n, :] + zbuf[k, 1, n, :] + zbuf[k, 2, n, :]
-            for j in (2, 1, 3):
+            pieces = 2 if k else 3
+            wait_received(zbuf.at[k, pl.ds(0, pieces), n], z_recv.at[k])
+            value = ct[k, n, lanes_of(z)]
+            for at in range(pieces):
+                value += zbuf[k, at, n, :]
+            zs[k, n, :] = value
+            for j in (2, 1, 3, 0):
                 part = pl.ds(pl.multiple_of(shifted(a, j) * size, size), size)
-                go(remote(zs.at[k, part], abuf.at[k, j - 1, q], a_send.at[k], a_recv.at[k], along_a(j)))
+                for core in (0, 1):
+                    if j or core:
+                        to = device(shifted(a, j), b, z, (c + core) % 2)
+                        go(remote(zs.at[k, part, half((c + core) % 2)], abuf.at[k, 2 * j + core - 1, q], a_send.at[k], a_recv.at[k], to))
             wait_sent(abuf.at[k, :, q], a_send.at[k])
         else:
             f = k - last + A_FIRST
@@ -234,32 +292,20 @@
         rows = pl.ds(starts[k], CHUNKS[k])
         o_ref[rows, :] = value
 
-    def reduce_second(k):
+    def finish(k):
         size = CHUNKS[k]
-        rows = pl.ds(starts[k], size)
         own = pl.ds(pl.multiple_of(a * size, size), size)
         q = pl.ds(0, size)
         if z_first[k]:
-            wait_received(abuf.at[k, :, q], a_recv.at[k])
-            asum[rows, :] = zs[k, own, :] + abuf[k, 0, q, :] + abuf[k, 1, q, :] + abuf[k, 2, q, :]
-            c_copies[k] = go(remote(asum.at[rows, half(1 - c)], cbuf.at[rows], c_send.at[k], c_recv.at[k], other_core))
-            sent.append(c_copies[k])
-
-    def finish(k):
-        size = CHUNKS[k]
-        rows = pl.ds(starts[k], size)
-        q = pl.ds(0, size)
-        if z_first[k]:
-            c_copies[k].wait_recv()
-            write(k, asum[rows, half(c)] + cbuf[rows, :])
+            parts, at_k, recv, value = abuf, k, a_recv, zs[k, own, half(c)]
         else:
             f = k - last + A_FIRST
-            own = pl.ds(pl.multiple_of(a * size, size), size)
+            parts, at_k, recv = zdirect, f, d_recv
             value = ct[k, own, pl.ds(pl.multiple_of(z * MZ + c * (MZ // 2), MZ // 2), MZ // 2)]
-            wait_received(zdirect.at[f, :, q], d_recv.at[f])
-            for at in range(7):
-                value += zdirect[f, at, q, :]
-            write(k, value)
+        wait_received(parts.at[at_k, :, q], recv.at[at_k])
+        for at in range(7):
+            value += parts[at_k, at, q, :]
+        o_ref[pl.ds(starts[k], size), :] = value
 
     gather(0, t_ref.at[:, columns(a)])
     send_v(0)
@@ -283,14 +329,17 @@
 
     for k in range(1, last):
         for later in range(2 if k == 1 else k + 2, min(k + 3, last)):
-            send_v(later)
+            if later < last - 1:
+                send_v(later)
+        if k == last - 3:
+            send_v_half(0)
+        if k == last - 2 - LATE:
+            send_v_half(1)
         all_tiles(k)
         if 2 <= k < last - A_FIRST + 1:
             reduce_first(k - 2)
     for k in range(last - A_FIRST - 1, last):
         reduce_first(k)
-    for k in range(last):
-        reduce_second(k)
     for k in range(last):
         finish(k)
     for copy in sent:
@@ -313,17 +362,16 @@
             pltpu.VMEM((SIDE * SIDE * TROWS, KQ), bf16),
             pltpu.VMEM((2 * SIDE * most, KQ), bf16),
             pltpu.VMEM((steps, SIDE * most, SIDE * MZ), f32),
+            pltpu.VMEM((steps, 2, SIDE * most // 2, MZ), f32),
             pltpu.VMEM((steps, SIDE - 1, SIDE * most, MZ), f32),
             pltpu.VMEM((steps, SIDE * most, MZ), f32),
-            pltpu.VMEM((steps, SIDE - 1, most, MZ), f32),
+            pltpu.VMEM((steps, 7, most, MZ // 2), f32),
             pltpu.VMEM((A_FIRST, SIDE - 1, most, SIDE * MZ), f32),
             pltpu.VMEM((A_FIRST, 7, most, MZ // 2), f32),
-            pltpu.VMEM((VROWS, MZ), f32),
-            pltpu.VMEM((VROWS, MZ // 2), f32),
             dma(()), dma((SIDE - 1,)),
             dma(()), dma((2 * SIDE,)),
             dma(()), dma((SIDE,)),
-            dma(()), dma((steps,)),
+            dma(()), dma((steps + 1,)),
             dma((steps - A_FIRST,)), dma((steps - A_FIRST,)),
             dma((steps - A_FIRST,)), dma((steps - A_FIRST,)),
             dma((A_FIRST,)), dma((A_FIRST,)),

time: 114 us -> 113 us (level)
    pallas_call x1, Pallas kernels: 113 us -> 112 us  [local(): pl.pallas_call(kernel, out_shape=pltpu.VMEM((VROWS, MZ // 2), f32), in_sp...]
where the time goes in v4:
time: 113 us
  Pallas kernels  112 us (99%)
    pallas_call x1, Pallas kernels, local(): pl.pallas_call(kernel, out_shape=pltpu.VMEM((VROWS, MZ // 2), f32), in_sp...  112 us

profile of v4, /device:TPU:1, one launch (start us, length us, event | category | flops | bytes accessed | tf_op | source)
XLA Modules:
  0.0 113.0 jit_solution(11342573212603230476)
XLA Ops:
  0.0 112.2 %shard_map.28 = f32[256,128]{1,0:T(8,128)S(1)} custom-call(f32[64,8192]{1,0:T(8,128)} %t_ref.1, f32[256,8192]{1,0:T(8,128)} %v_ref.1), custom_call_target="tpu_custom_call" | custom-call | flops 12884901888 | bytes 10485760 | tf_op jit(solution)/shard_map/pallas_call | solution.py:353
  112.2 0.8 copy.3

commit v5 on v4

--- a/solution.py
+++ b/solution.py
@@ -12,8 +12,9 @@
 TROWS = 64
 VROWS = 256
 MZ = 256
-CHUNKS = (64, 64, 64, 32, 32)
+CHUNKS = (64, 64, 48, 48, 32)
 LATE = 1
+DELAY = 1
 A_FIRST = 2
 VMEM_BYTES = 60 << 20
 
@@ -244,16 +245,19 @@
 
         if z_first[k]:
             wait_sent(zh.at[k, :, pl.ds(0, n // 2)], h_send.at[k])
-            wait_received(zh.at[k, :, pl.ds(0, n // 2)], h_recv.at[k])
-            for w in (0, 1):
-                m = lanes_of(shifted(z, 1 - 2 * w))
-                rows = pl.ds(0, n)
-                ct[k, pl.ds(w * n // 2, n // 2), m] += zh[k, w, pl.ds(0, n // 2), :]
-                go(remote(ct.at[k, rows, m], zbuf.at[k, w, rows], z_send.at[k], z_recv.at[k], along_z(1 - 2 * w)))
-            wait_sent(zbuf.at[k, pl.ds(0, 2), pl.ds(0, n)], z_send.at[k])
         else:
             f = k - last + A_FIRST
             wait_sent(afirst.at[f, :, pl.ds(0, CHUNKS[k])], b_send.at[f])
+
+    def onward_z(k):
+        n = SIDE * CHUNKS[k]
+        wait_received(zh.at[k, :, pl.ds(0, n // 2)], h_recv.at[k])
+        for w in (0, 1):
+            m = lanes_of(shifted(z, 1 - 2 * w))
+            rows = pl.ds(0, n)
+            ct[k, pl.ds(w * n // 2, n // 2), m] += zh[k, w, pl.ds(0, n // 2), :]
+            go(remote(ct.at[k, rows, m], zbuf.at[k, w, rows], z_send.at[k], z_recv.at[k], along_z(1 - 2 * w)))
+        wait_sent(zbuf.at[k, pl.ds(0, 2), pl.ds(0, n)], z_send.at[k])
 
     def reduce_first(k):
         size = CHUNKS[k]
@@ -336,9 +340,11 @@
         if k == last - 2 - LATE:
             send_v_half(1)
         all_tiles(k)
-        if 2 <= k < last - A_FIRST + 1:
-            reduce_first(k - 2)
-    for k in range(last - A_FIRST - 1, last):
+        if k < last - A_FIRST and not (DELAY and k == last - A_FIRST - 1):
+            onward_z(k)
+        if DELAY and k == last - A_FIRST:
+            onward_z(k - 1)
+    for k in [0, 1, last - 2, last - 3, last - 1]:
         reduce_first(k)
     for k in range(last):
         finish(k)

time: 113 us -> 112 us (level)
    pallas_call x1, Pallas kernels: 112 us -> 111 us  [local(): pl.pallas_call(kernel, out_shape=pltpu.VMEM((VROWS, MZ // 2), f32), in_sp...]
where the time goes in v5:
time: 112 us
  Pallas kernels  111 us (99%)
    pallas_call x1, Pallas kernels, local(): pl.pallas_call(kernel, out_shape=pltpu.VMEM((VROWS, MZ // 2), f32), in_sp...  111 us

profile of v5, /device:TPU:1, one launch (start us, length us, event | category | flops | bytes accessed | tf_op | source)
XLA Modules:
  0.0 111.7 jit_solution(3207322928552480809)
XLA Ops:
  0.0 111.0 %shard_map.28 = f32[256,128]{1,0:T(8,128)S(1)} custom-call(f32[64,8192]{1,0:T(8,128)} %t_ref.1, f32[256,8192]{1,0:T(8,128)} %v_ref.1), custom_call_target="tpu_custom_call" | custom-call | flops 12884901888 | bytes 10485760 | tf_op jit(solution)/shard_map/pallas_call | solution.py:359
  111.0 0.8 copy.3

commit v6 on v5

--- a/solution.py
+++ b/solution.py
@@ -234,6 +234,10 @@
         def _(step):
             j = (step + 2) % SIDE if z_first[k] else (step + 1) % SIDE
             multiply(k, lanes_of(shifted(z, j)))
+            if k == last - A_FIRST:
+                @pl.when(step == 1)
+                def _():
+                    onward_z(k - 1)
             if z_first[k]:
                 @pl.when(step == 0)
                 def _():
@@ -245,6 +249,7 @@
 
         if z_first[k]:
             wait_sent(zh.at[k, :, pl.ds(0, n // 2)], h_send.at[k])
+            wait_sent(zbuf.at[k, pl.ds(0, 2), pl.ds(0, n)], z_send.at[k])
         else:
             f = k - last + A_FIRST
             wait_sent(afirst.at[f, :, pl.ds(0, CHUNKS[k])], b_send.at[f])
@@ -257,7 +262,6 @@
             rows = pl.ds(0, n)
             ct[k, pl.ds(w * n // 2, n // 2), m] += zh[k, w, pl.ds(0, n // 2), :]
             go(remote(ct.at[k, rows, m], zbuf.at[k, w, rows], z_send.at[k], z_recv.at[k], along_z(1 - 2 * w)))
-        wait_sent(zbuf.at[k, pl.ds(0, 2), pl.ds(0, n)], z_send.at[k])
 
     def reduce_first(k):
         size = CHUNKS[k]
@@ -326,24 +330,22 @@
     forward(1)
     forward(3)
     forward(2)
-    send_v(1)
     pl.loop(0, SIDE)(convert_sides)
     convert_v(0)
+    send_v(1)
     early_tiles()
 
     for k in range(1, last):
         for later in range(2 if k == 1 else k + 2, min(k + 3, last)):
             if later < last - 1:
                 send_v(later)
-        if k == last - 3:
+        if k == 1:
             send_v_half(0)
         if k == last - 2 - LATE:
             send_v_half(1)
         all_tiles(k)
         if k < last - A_FIRST and not (DELAY and k == last - A_FIRST - 1):
             onward_z(k)
-        if DELAY and k == last - A_FIRST:
-            onward_z(k - 1)
     for k in [0, 1, last - 2, last - 3, last - 1]:
         reduce_first(k)
     for k in range(last):

time: 112 us -> 112 us (level)
  no operation moved by 1% of the time
where the time goes in v6:
time: 112 us
  Pallas kernels  111 us (99%)
    pallas_call x1, Pallas kernels, local(): pl.pallas_call(kernel, out_shape=pltpu.VMEM((VROWS, MZ // 2), f32), in_sp...  111 us

profile of v6, /device:TPU:1, one launch (start us, length us, event | category | flops | bytes accessed | tf_op | source)
XLA Modules:
  0.0 111.6 jit_solution(11243920001218422377)
XLA Ops:
  0.0 110.8 %shard_map.28 = f32[256,128]{1,0:T(8,128)S(1)} custom-call(f32[64,8192]{1,0:T(8,128)} %t_ref.1, f32[256,8192]{1,0:T(8,128)} %v_ref.1), custom_call_target="tpu_custom_call" | custom-call | flops 12884901888 | bytes 10485760 | tf_op jit(solution)/shard_map/pallas_call | solution.py:361
  110.8 0.8 copy.3
